TPU v7x, 32 devices: a whole 2x2x4 slice. The times are simulated.
32 devices in a mesh: users: 8 (over z, x), items: 4 (over y, core).
Axes of the slice: x: 2, y: 2, z: 4, core: 2. Of those that a mesh axis runs over, the one named last changes fastest.
Arguments:
- interactions: bfloat16 [16384, 32768], P('users', 'items'), may hold values from 0 to 13, as said below
- user_weights: bfloat16 [16384], P('users'), may hold values from 0.3 to 9, as said below
- panel_index: int32 [1], replicated, may hold values from 0 to 127
Outputs:
- item_covariance: float32 [32, 1024, 256], P(None, ('users', 'items'))
- item_mean: float32 [32, 1024], P(None, ('users', 'items'))
Inputs may be any that keep to these rules, and one draw needn't show every extreme that they name: `user_weights`: positive user weights. `interactions`: confidences are zero or positive.
All inputs are finite; a program needn't handle non-finite values.
Results may differ from a plain program's by a relative error of at most 0.00031.
Values may be sent and summed in bfloat16 or wider, within the bound.
A program may use at most 384 MiB of HBM per device.

v0:
```python
import jax
import jax.numpy as jnp
from jax import lax
from jax.sharding import PartitionSpec as P

P_SIZE = 256
BLK = 32


def from_root(block, axis, source):
    block = jnp.where(lax.axis_index(axis) == source, block, jnp.zeros_like(block))
    return lax.psum(block, axis)


def combined_all(value, axis, join):
    pieces = jax.tree.map(lambda part: lax.all_gather(part, axis), value)
    head = jax.tree.map(lambda part: part[0], pieces)
    tail = jax.tree.map(lambda part: part[1:], pieces)
    total, _ = lax.scan(lambda total, slab: (join(total, slab), None), head, tail)
    return total


def chan_combine(left, right):
    count_a, mean_a, panel_a, moment_a = left
    count_b, mean_b, panel_b, moment_b = right
    total = count_a + count_b
    factor = count_b / total
    delta = mean_b - mean_a
    panel_delta = panel_b - panel_a
    moment = moment_a + moment_b + count_a * count_b / total * delta[:, None] * panel_delta[None, :]
    return (total, mean_a + factor * delta, panel_a + factor * panel_delta, moment)


def contract_users(left, right):
    return lax.dot_general(
        left, right, (((0,), (0,)), ((), ())), preferred_element_type=jnp.float32
    )


def per_device(interactions, user_weights, panel_index):
    shard_rows = interactions.shape[1]
    per_shard = shard_rows // P_SIZE
    chosen = panel_index[0]
    owner = chosen // per_shard
    local_cols = lax.dynamic_slice_in_dim(interactions, chosen % per_shard * P_SIZE, P_SIZE, 1)
    panel = from_root(local_cols, "items", owner)
    weights32 = user_weights.astype(jnp.float32)
    weighted = (weights32[:, None] * panel.astype(jnp.float32)).astype(jnp.bfloat16)
    gram = contract_users(interactions, weighted)
    colsum = contract_users(interactions, user_weights)
    panel_sum = contract_users(user_weights, panel)
    count = jnp.sum(weights32).reshape(1)
    users_count = lax.axis_size("users")
    items_count = lax.axis_size("items")
    cycles_local = shard_rows // (users_count * items_count * BLK)
    tile_shape = (cycles_local, users_count, items_count, BLK, P_SIZE)
    mean_local = colsum / count
    panel_local = panel_sum / count
    moment = gram - mean_local[:, None] * panel_sum[None, :]
    total, mean_all, panel_all, moment_all = combined_all(
        (count, mean_local, panel_local, moment), "users", chan_combine
    )
    rank = lax.axis_index("users")
    own_moment = lax.dynamic_slice_in_dim(moment_all.reshape(tile_shape), rank, 1, 1)
    covar = own_moment / total
    mean_part = lax.dynamic_slice_in_dim(mean_all.reshape(tile_shape[:4]), rank, 1, 1)
    moved_cov, moved_mean = (
        lax.all_to_all(covar, "items", split_axis=2, concat_axis=0, tiled=True),
        lax.all_to_all(mean_part, "items", split_axis=2, concat_axis=0, tiled=True),
    )
    return (moved_cov.reshape(-1, BLK, P_SIZE), moved_mean.reshape(-1, BLK))


def solution(mesh):
    return jax.shard_map(
        per_device,
        mesh=mesh,
        in_specs=(P("users", "items"), P("users"), P()),
        out_specs=(P(None, ("users", "items"), None), P(None, ("users", "items"))),
        check_vma=False,
    )
```

profile of v0, /device:TPU:0, one launch (start us, length us, event | category | flops | bytes accessed | tf_op | source)
XLA Modules:
  0.0 1586.0 jit_solution(3609545199093069631)
XLA Ops:
  7.2 0.0 all-reduce.3.cloned.1.call-start
  7.9 2.4 dynamic-slice_select_fusion
  10.3 0.0 all-reduce.3.cloned.1.call-update
  10.3 0.0 all-gather.6.cloned.1.call-start
  10.4 0.7 reshape.62
  11.0 0.0 copy-start.1
  11.1 13.0 fusion.3
  24.1 0.0 copy-done.1
  24.1 0.6 convert_reduce_fusion
  24.7 0.7 broadcast_divide_fusion
  25.4 24.4 %all-reduce.3.cloned.1.call-done = bf16[2048,256]{1,0:T(8,128)(2,1)} async-done(((bf16[2048,256]{1,0:T(8,128)(2,1)}), bf16[2048,256]{1,0:T(8,128)(2,1)}) %all-reduce.3.cloned.1.call-update) | async-done | bytes 1048592 | tf_op jit(solution)/shard_map/psum | solution.py:12
  49.8 1.5 fusion.4
  51.3 17.6 %fusion.1 = f32[8192,256]{0,1:T(8,128)} fusion(bf16[2048,8192]{1,0:T(8,128)(2,1)} %param.5, f32[256]{0:T(256)S(1)} %bitcast.74, f32[8192]{0:T(1024)S(1)} %broadcast_divide_fusion, bf16[2048,256]{1,0:T(8,128)(2,1)} %all-reduce.3.cloned.1.call-done, f32[2048]{0:T(1024)S(1)} %convert_element_type.9), kind=kOutput, calls=%fused_computation.9 | convolution fusion | flops 8595701760 | bytes 43033600 | tf_op jit(solution)/shard_map/dot_general | solution.py:35
  68.8 0.0 copy-start.3
  68.8 0.0 all-gather.6.cloned.1.call-update
  68.9 0.6 copy-done.3
  69.5 0.6 dynamic-slice
  70.1 1.4 dynamic-update-slice
  71.5 109.3 %all-reduce = f32[8]{0:T(128)} all-reduce(f32[8]{0:T(128)S(1)} %dynamic-update-slice), channel_id=1, replica_groups=mesh['users'=8,'items'=4] {'users'}, use_global_device_ids=true, to_apply=%add | all-reduce | flops 8 | bytes 64
  180.8 50.8 %all-gather = f32[65536]{0:T(1024)S(1)} all-gather(f32[8192]{0:T(1024)S(1)} %broadcast_divide_fusion), channel_id=2, replica_groups=mesh['users'=8,'items'=4] {'users'}, dimensions={0}, use_global_device_ids=true | all-gather | bytes 294912 | tf_op jit(solution)/shard_map/all_gather | solution.py:16
  231.6 0.0 copy-start
  231.7 0.7 slice_bitcast_fusion
  232.4 0.6 broadcast_divide_fusion.1
  233.0 35.5 %all-gather.3 = f32[8,1,256]{2,1,0:T(1,128)S(1)} all-gather(f32[1,1,256]{2,1,0:T(1,128)S(1)} %bitcast.76), channel_id=3, replica_groups=mesh['users'=8,'items'=4] {'users'}, dimensions={0}, use_global_device_ids=true | all-gather | bytes 9216 | tf_op jit(solution)/shard_map/all_gather | solution.py:16
  268.5 0.0 copy-start.2
  268.5 1073.4 %all-gather.6.cloned.1.call-done = f32[65536,256]{0,1:T(8,128)} async-done(((f32[8192,256]{0,1:T(8,128)}), f32[65536,256]{0,1:T(8,128)}) %all-gather.6.cloned.1.call-update) | async-done | bytes 67108880 | tf_op jit(solution)/shard_map/all_gather | solution.py:16
  1341.9 7.5 slice.44
  1349.4 0.0 copy-done
  1349.4 0.0 copy-done.2
  1349.4 9.0 copy.19
  1358.4 39.3 %slice.47 = f32[57344,256]{0,1:T(8,128)} slice(f32[65536,256]{0,1:T(8,128)} %all-gather.6.cloned.1.call-done), slice={[8192:65536], [0:256]} | slice | bytes 117440512 | tf_op jit(solution)/shard_map/slice | solution.py:18
  1397.7 0.0 slice-start
  1397.7 0.0 slice-start.1
  1397.7 57.7 %copy.18 = f32[57344,256]{1,0:T(8,128)} copy(f32[57344,256]{0,1:T(8,128)} %slice.47) | data formatting | bytes 117440512 | tf_op jit(solution)/shard_map/slice | solution.py:18
  1455.3 0.0 slice-done
  1455.3 0.0 slice-done.1
  1455.3 95.8 %while.16 = (s32[]{:T(128)}, f32[1]{0:T(128)}, f32[8192]{0:T(1024)S(1)}, f32[256]{0:T(256)S(1)}, f32[8192,256]{1,0:T(8,128)}, /*index=5*/f32[7,1]{0,1:T(1,128)S(...) while((s32[]{:T(128)}, f32[1]{0:T(128)}, f32[8192]{0:T(1024)S(1)}, ...), condition=%wide.region_3.4_spmd, body=%wide.region_2.3_spmd.sunk | while | flops 6324998 | bytes 25402568 | solution.py:19
  1455.9 0.6 constant_dynamic-slice_fusion.7
  1458.6 9.9 fusion.11
  1469.6 0.6 constant_dynamic-slice_fusion.7
  1472.3 9.9 fusion.11
  1483.3 0.6 constant_dynamic-slice_fusion.7
  1485.9 9.9 fusion.11
  1496.9 0.6 constant_dynamic-slice_fusion.7
  1499.6 9.9 fusion.11
  1510.6 0.6 constant_dynamic-slice_fusion.7
  1513.3 9.9 fusion.11
  1524.3 0.6 constant_dynamic-slice_fusion.7
  1527.0 9.9 fusion.11
  1538.0 0.6 constant_dynamic-slice_fusion.7
  1540.7 9.9 fusion.11
  1551.1 0.1 reshape.34
  1551.3 0.6 broadcast.12
  1551.9 0.7 reduce
  1552.6 0.7 reshape.66
  1553.3 3.2 all-to-all-start.1
  1556.5 1.9 dynamic-slice_divide_fusion
  1558.5 1.1 copy.20
  1559.6 0.7 all-to-all-done.1
  1560.3 3.5 all-to-all-start
  1563.8 0.7 reduce.1
  1564.5 0.7 reshape.67
  1565.2 13.0 all-to-all-done
  1578.2 1.0 copy.47
  (36 shorter events, 0.6 us)
Async XLA Ops:
  7.2 42.6 %all-reduce.3.cloned.1.call-start = ((), (), s32[]{:S(2)}) async-start(), calls=%async_computation.2 | async-start | bytes 2097152 | tf_op jit(solution)/shard_map/psum | solution.py:12
  10.3 1331.6 %all-gather.6.cloned.1.call-start = ((), (), s32[]{:S(2)}) async-start(), calls=%async_computation.3 | async-start | bytes 75497472 | tf_op jit(solution)/shard_map/all_gather | solution.py:16
  11.0 13.0 copy-start.1
  68.8 0.7 copy-start.3
  231.6 1117.8 %copy-start = (f32[65536]{0:T(1024)}, f32[65536]{0:T(1024)S(1)}, u32[]{:S(2)}) copy-start(f32[65536]{0:T(1024)S(1)} %all-gather) | copy-start | bytes 786436
  268.5 1080.9 %copy-start.2 = (f32[8,1,256]{2,1,0:T(1,128)}, f32[8,1,256]{2,1,0:T(1,128)S(1)}, u32[]{:S(2)}) copy-start(f32[8,1,256]{2,1,0:T(1,128)S(1)} %all-gather.3) | copy-start | bytes 24580
  1397.7 57.7 %slice-start = ((f32[65536]{0:T(1024)}), f32[8192]{0:T(1024)S(1)}, s32[]{:S(2)}) async-start(f32[65536]{0:T(1024)} %copy-done), calls=%async_computation.4 | async-start | bytes 65536 | tf_op jit(solution)/shard_map/slice | solution.py:17
  1397.7 57.7 %slice-start.1 = ((f32[8,1,256]{2,1,0:T(1,128)}), f32[1,1,256]{2,1,0:T(1,128)S(1)}, s32[]{:S(2)}) async-start(f32[8,1,256]{2,1,0:T(1,128)} %copy-done.2), calls=%async_computation.5 | async-start | bytes 2048 | tf_op jit(solution)/shard_map/slice | solution.py:17
  1553.3 7.0 all-to-all-start.1
  1560.3 18.0 %all-to-all-start = ((f32[8,1,4,32,256]{4,3,0,1,2:T(8,128)}), f32[8,1,4,32,256]{4,3,0,1,2:T(8,128)S(1)}, u32[]{:S(2)}, u32[]{:S(2)}) async-start(f32[8,1,4,32,256]{4,3,0,1,2:T(8,128)} %copy.20), calls=%async_computation | async-start | bytes 2097152 | tf_op jit(solution)/shard_map/all_to_all | solution.py:68
Sparse Core Ops, SparseCore 0:
  10.9 38.8 all-reduce.2
  69.0 1272.8 all-gather.5
where the time goes:
time: 1590 us
  waiting for transfers between devices  1110 us (70%)
  blocking collectives  196 us (12%)
  local copies, waits for them, and re-layouts  126 us (8%)
  other arithmetic  77.3 us (5%)
  matrix products  32.1 us (2%)
  loops' own time  21.8 us (1%)
    all_gather x1, waiting for transfers between devices, combined_all(): pieces = jax.tree.map(lambda part: lax.all_gather(part, axis), value)  1070 us
    unnamed x1, blocking collectives  109 us
    slice x6, local copies, waits for them, and re-layouts, combined_all(): tail = jax.tree.map(lambda part: part[1:], pieces)  97.7 us
    all_gather x2, blocking collectives, combined_all(): pieces = jax.tree.map(lambda part: lax.all_gather(part, axis), value)  86.3 us
    add x7, other arithmetic, chan_combine(): moment_a + moment_b  69.4 us
    dot_general x3, matrix products, contract_users(): lax.dot_general(left, right, (((0,), (0,)), ((), ())), preferred_element_...  32.1 us
  transfers between devices with their start and end apart: 4, of which 4 were waited for; matrix products, arithmetic and copies ran while one was open for 1% of the time, Pallas kernels for 0%

commit v1 on v0

v1 whole, which is shorter than its diff:
```python
import functools
import math

import jax
import jax.numpy as jnp
from jax import lax
from jax.experimental import pallas as pl
from jax.experimental.pallas import tpu as pltpu
from jax.sharding import PartitionSpec as P

P_SIZE = 256
BLK = 32
EXTRA = 16
TILE = 256
PIECES = 4
LAG = 3
STEP = math.log(2.0) / 256.0
TOP = 32600.0
f32 = jnp.float32


def encode(block):
    top = jnp.max(jnp.abs(block), axis=0, keepdims=True)
    code = jnp.ceil(jnp.log(jnp.maximum(top, 1e-30)) * (1.0 / STEP)) + 1.0
    scaled = jnp.round(block * (jnp.exp(code * -STEP) * TOP))
    codes = jnp.broadcast_to(code, (EXTRA, block.shape[1]))
    return scaled.astype(jnp.int32).astype(jnp.int16), codes.astype(jnp.int32).astype(jnp.int16)


def decode(ref):
    code = ref[P_SIZE : P_SIZE + EXTRA, :].astype(jnp.int32).astype(f32)[0:1]
    return ref[0:P_SIZE, :].astype(jnp.int32).astype(f32) * (jnp.exp(code * STEP) * (1.0 / TOP))


def kernel(
    sizes, x_ref, loc_ref, w_ref, cov_ref, mean_ref,
    xbuf, turned, full, half, near, far, lhs, pmean, gram, own,
    xsend, xrecv, zsend, zrecv, icov, sums, sums_all, stat, stat_all, shift, mean_mine, mean_all,
    load_sem, near_s, near_r, far_s, far_r, back_s, back_r, xs, xr, zs, zr, is_, ir,
    sum_s, sum_r, stat_s, stat_r, mean_s, mean_r,
):
    users, items, xn, zn, cyc, width = sizes
    rows = loc_ref.shape[0]
    chunk = users * width
    user, item = lax.axis_index("users"), lax.axis_index("items")
    z, x = lax.div(user, xn), lax.rem(user, xn)
    y, core = lax.div(item, 2), lax.rem(item, 2)
    yn = items // 2

    def load(c):
        return pltpu.make_async_copy(x_ref.at[:, pl.ds(c * chunk, chunk)], xbuf.at[c], load_sem.at[c])

    def remote(src, dst, send, recv, to_user, to_item):
        return pltpu.make_async_remote_copy(
            src_ref=src, dst_ref=dst, send_sem=send, recv_sem=recv,
            device_id={"users": to_user, "items": to_item},
            device_id_type=pl.DeviceIdType.MESH,
        )

    for c in range(cyc):
        load(c).start()

    barrier = pltpu.get_barrier_semaphore()
    for d in range(1, users):
        pl.semaphore_signal(
            barrier, inc=1, device_id={"users": lax.rem(user + d, users), "items": item},
            device_id_type=pl.DeviceIdType.MESH,
        )
    for d in range(1, items):
        pl.semaphore_signal(
            barrier, inc=1, device_id={"users": user, "items": lax.rem(item + d, items)},
            device_id_type=pl.DeviceIdType.MESH,
        )
    for r in range(rows // TILE):
        part = pl.ds(r * TILE, TILE)
        turned[:, part] = loc_ref[part, :].astype(f32).T.astype(jnp.bfloat16)
    pl.semaphore_wait(barrier, users + items - 2)

    side = P_SIZE // 2
    piece = side // PIECES

    def near_copy(p):
        start = pl.multiple_of((1 - core) * side + p * piece, piece)
        return remote(turned.at[pl.ds(start, piece)], near.at[pl.ds(p * piece, piece)],
                      near_s.at[p], near_r.at[p], user, y * 2 + 1 - core)

    def far_copy(p, d):
        return remote(half.at[pl.ds(p * piece, piece)], far.at[d - 1, pl.ds(p * piece, piece)],
                      far_s.at[p, d - 1], far_r.at[p, d - 1], user, lax.rem(y + d, yn) * 2 + core)

    def back_copy(p):
        start = pl.multiple_of(core * side + p * piece, piece)
        return remote(full.at[pl.ds(start, piece)], full.at[pl.ds(start, piece)],
                      back_s.at[p], back_r.at[p], user, y * 2 + 1 - core)

    for p in range(PIECES):
        near_copy(p).start()
    for p in range(PIECES):
        near_copy(p).wait_recv()
        mine = pl.ds(pl.multiple_of(core * side + p * piece, piece), piece)
        here = pl.ds(p * piece, piece)
        half[here, :] = turned[mine, :] + near[here, :]
        for d in range(1, yn):
            far_copy(p, d).start()
    for p in range(PIECES):
        here = pl.ds(p * piece, piece)
        value = half[here, :]
        for d in range(1, yn):
            far_copy(p, d).wait_recv()
            value = value + far[d - 1, here, :]
        full[pl.ds(pl.multiple_of(core * side + p * piece, piece), piece), :] = value
        back_copy(p).start()
    for p in range(PIECES):
        back_copy(p).wait_recv()

    weights = w_ref[...]
    count = jnp.sum(weights, axis=1, keepdims=True)
    for r in range(P_SIZE // 64):
        part = pl.ds(r * 64, 64)
        product = full[part, :].astype(f32) * weights
        lhs[part, :] = product.astype(jnp.bfloat16)
        pmean[part, :] = jnp.broadcast_to(jnp.sum(product, axis=1, keepdims=True), (64, 128))
    lhs[P_SIZE : P_SIZE + EXTRA, :] = jnp.broadcast_to(weights, (EXTRA, rows)).astype(jnp.bfloat16)
    stat[0:8, :] = pmean[...].T[0:8, :]
    stat[8:16, :] = jnp.broadcast_to(count, (8, P_SIZE))
    pmean[...] = pmean[...] / count

    def stat_copy(d):
        return remote(stat, stat_all.at[user], stat_s.at[d - 1], stat_r.at[d - 1],
                      lax.rem(user + d, users), item)

    for d in range(1, users):
        stat_copy(d).start()

    def x_copy(c, d):
        return remote(xsend.at[c, d - 1], xrecv.at[c, d - 1], xs.at[c, d - 1], xr.at[c, d - 1],
                      z * xn + lax.rem(x + d, xn), item)

    def z_copy(c, d):
        return remote(zsend.at[c, d - 1], zrecv.at[c, d - 1], zs.at[c, d - 1], zr.at[c, d - 1],
                      lax.rem(z + d, zn) * xn + x, item)

    def item_copy(c, d):
        peer = lax.rem(item + d, items)
        return remote(icov.at[c, pl.ds(pl.multiple_of(peer * BLK, BLK), BLK)],
                      cov_ref.at[item * cyc + c],
                      is_.at[c, d - 1], ir.at[c, d - 1], user, peer)

    def compute(c):
        load(c).wait()

        def tile(t, _):
            part = pl.ds(pl.multiple_of(t * TILE, TILE), TILE)
            value = jnp.dot(lhs[...], xbuf[c, :, part], preferred_element_type=f32)
            total = value[P_SIZE : P_SIZE + 1, :]
            gram[:, part] = value[0:P_SIZE, :] - pmean[:, 0:1] * total
            for b in range(TILE // width):
                sums[t * (TILE // width) + b, pl.ds(c, 1), :] = total[:, b * width : (b + 1) * width]
            return 0

        lax.fori_loop(0, chunk // TILE, tile, 0)
        for d in range(1, xn):
            for k in range(zn):
                start = pl.multiple_of((k * xn + lax.rem(x + d, xn)) * width, width)
                part = pl.ds(k * width, width)
                codes, scales = encode(gram[:, pl.ds(start, width)])
                xsend[c, d - 1, 0:P_SIZE, part] = codes
                xsend[c, d - 1, P_SIZE : P_SIZE + EXTRA, part] = scales
            x_copy(c, d).start()
        for k in range(zn):
            start = pl.multiple_of((k * xn + x) * width, width)
            own[c, :, pl.ds(k * width, width)] = gram[:, pl.ds(start, width)]

    def relay(c):
        for d in range(1, xn):
            x_copy(c, d).wait_recv()
            own[c] = own[c] + decode(xrecv.at[c, d - 1])
        for d in range(1, zn):
            start = pl.multiple_of(lax.rem(z + d, zn) * width, width)
            codes, scales = encode(own[c, :, pl.ds(start, width)])
            zsend[c, d - 1, 0:P_SIZE, :] = codes
            zsend[c, d - 1, P_SIZE : P_SIZE + EXTRA, :] = scales
            z_copy(c, d).start()

    lag = min(LAG, cyc)

    def first(c, _):
        compute(c)

        @pl.when(c >= lag)
        def _():
            relay(c - lag)

        return 0

    lax.fori_loop(0, cyc, first, 0)

    def sum_copy(d):
        peer = lax.rem(user + d, users)
        return remote(sums.at[peer], sums_all.at[user], sum_s.at[d - 1], sum_r.at[d - 1], peer, item)

    for d in range(1, users):
        sum_copy(d).start()
    sums_all[user] = sums[user]
    stat_all[user] = stat[...]
    for d in range(1, users):
        stat_copy(d).wait_recv()
    whole = stat_all[0]
    for g in range(1, users):
        whole = whole + stat_all[g]
    total = whole[8:9, 0:1]
    panel_mean = whole[0:1, :] / whole[8:9, :]
    for g in range(users):
        delta = stat_all[g, 0:1, :] / stat_all[g, 8:9, :] - panel_mean
        shift[g] = jnp.broadcast_to(delta, (width, P_SIZE)).T
    for d in range(1, users):
        sum_copy(d).wait_recv()
    means = sums_all[0]
    for g in range(1, users):
        means = means + sums_all[g]
    mean_mine[...] = means / total

    def mean_copy(d):
        return remote(mean_mine, mean_all.at[item], mean_s.at[d - 1], mean_r.at[d - 1],
                      user, lax.rem(item + d, items))

    for d in range(1, items):
        mean_copy(d).start()
    mean_all[item] = mean_mine[...]

    def finish(c):
        value = own[c, :, pl.ds(pl.multiple_of(z * width, width), width)]
        for g in range(users):
            value = value + shift[g] * sums_all[g, pl.ds(c, 1), :]
        for d in range(1, zn):
            z_copy(c, d).wait_recv()
            value = value + decode(zrecv.at[c, d - 1])
        icov[c] = (value / total).T
        for d in range(1, items):
            item_copy(c, d).start()
        cov_ref[item * cyc + c] = icov[c, pl.ds(pl.multiple_of(item * BLK, BLK), BLK), :]

    def second(c, _):
        @pl.when(c < lag)
        def _():
            relay(cyc - lag + c)

        finish(c)
        return 0

    lax.fori_loop(0, cyc, second, 0)

    for d in range(1, items):
        mean_copy(d).wait()
    for i in range(items):
        value = jnp.zeros(mean_ref.shape[1:], f32)
        for k in range(items):
            value = jnp.where(item == k, mean_all[i, :, k * BLK : (k + 1) * BLK], value)
        mean_ref[i] = value

    for p in range(PIECES):
        near_copy(p).wait_send()
        back_copy(p).wait_send()
        for d in range(1, yn):
            far_copy(p, d).wait_send()
    for d in range(1, users):
        stat_copy(d).wait_send()
        sum_copy(d).wait_send()

    def drain(c, _):
        for d in range(1, xn):
            x_copy(c, d).wait_send()
        for d in range(1, zn):
            z_copy(c, d).wait_send()
        for d in range(1, items):
            item_copy(c, d).wait()
        return 0

    lax.fori_loop(0, cyc, drain, 0)


def per_device(interactions, user_weights, panel_index):
    rows, shard = interactions.shape
    users, items = lax.axis_size("users"), lax.axis_size("items")
    zn = 4 if users % 4 == 0 else 1
    xn = users // zn
    width = items * BLK
    cyc = shard // (users * width)
    cyc8 = -(-cyc // 8) * 8
    yn = items // 2
    per_shard = shard // P_SIZE
    chosen = panel_index[0]
    local = lax.dynamic_slice_in_dim(interactions, chosen % per_shard * P_SIZE, P_SIZE, 1)
    local = jnp.where(lax.axis_index("items") == chosen // per_shard, local, jnp.zeros_like(local))
    weights = user_weights.astype(f32)[None, :]

    bf16, i16 = jnp.bfloat16, jnp.int16
    side, tall = P_SIZE // 2, P_SIZE + EXTRA
    dma = pltpu.SemaphoreType.DMA
    vmem = pl.BlockSpec(memory_space=pltpu.VMEM)
    cov, mean = pl.pallas_call(
        functools.partial(kernel, (users, items, xn, zn, cyc, width)),
        out_shape=(
            jax.ShapeDtypeStruct((items * cyc, BLK, P_SIZE), f32),
            jax.ShapeDtypeStruct((items, cyc8, BLK), f32),
        ),
        in_specs=[pl.BlockSpec(memory_space=pl.ANY), vmem, vmem],
        out_specs=(vmem, vmem),
        scratch_shapes=[
            pltpu.VMEM((cyc, rows, users * width), bf16),
            pltpu.VMEM((P_SIZE, rows), bf16),
            pltpu.VMEM((P_SIZE, rows), bf16),
            pltpu.VMEM((side, rows), bf16),
            pltpu.VMEM((side, rows), bf16),
            pltpu.VMEM((yn - 1, side, rows), bf16),
            pltpu.VMEM((tall, rows), bf16),
            pltpu.VMEM((P_SIZE, 128), f32),
            pltpu.VMEM((P_SIZE, users * width), f32),
            pltpu.VMEM((cyc, P_SIZE, zn * width), f32),
            pltpu.VMEM((cyc, xn - 1, tall, zn * width), i16),
            pltpu.VMEM((cyc, xn - 1, tall, zn * width), i16),
            pltpu.VMEM((cyc, zn - 1, tall, width), i16),
            pltpu.VMEM((cyc, zn - 1, tall, width), i16),
            pltpu.VMEM((cyc, width, P_SIZE), f32),
            pltpu.VMEM((users, cyc8, width), f32),
            pltpu.VMEM((users, cyc8, width), f32),
            pltpu.VMEM((16, P_SIZE), f32),
            pltpu.VMEM((users, 16, P_SIZE), f32),
            pltpu.VMEM((users, P_SIZE, width), f32),
            pltpu.VMEM((cyc8, width), f32),
            pltpu.VMEM((items, cyc8, width), f32),
            dma((cyc,)),
            dma((PIECES,)), dma((PIECES,)),
            dma((PIECES, yn - 1)), dma((PIECES, yn - 1)),
            dma((PIECES,)), dma((PIECES,)),
            dma((cyc, xn - 1)), dma((cyc, xn - 1)),
            dma((cyc, zn - 1)), dma((cyc, zn - 1)),
            dma((cyc, items - 1)), dma((cyc, items - 1)),
            dma((users - 1,)), dma((users - 1,)),
            dma((users - 1,)), dma((users - 1,)),
            dma((items - 1,)), dma((items - 1,)),
        ],
        compiler_params=pltpu.CompilerParams(
            collective_id=0, has_side_effects=True, vmem_limit_bytes=60 * 2**20
        ),
        cost_estimate=pl.CostEstimate(
            flops=2 * tall * rows * shard, bytes_accessed=2 * rows * shard, transcendentals=0
        ),
        name="panel_covariance",
    )(interactions, local, weights)
    return cov, mean[:, :cyc].reshape(items * cyc, BLK)


def solution(mesh):
    return jax.shard_map(
        per_device,
        mesh=mesh,
        in_specs=(P("users", "items"), P("users"), P()),
        out_specs=(P(None, ("users", "items"), None), P(None, ("users", "items"))),
        check_vma=False,
    )
```

time: 1590 us -> 109 us (0.07)
  waiting for transfers between devices: 1110 us -> 0 us
  blocking collectives: 196 us -> 0 us
  local copies, waits for them, and re-layouts: 126 us -> 3.63 us
  Pallas kernels: 0 us -> 100 us
  other arithmetic: 77.3 us -> 3.66 us
  matrix products: 32.1 us -> 0 us
  loops' own time: 21.8 us -> 0 us
    all_gather x1 -> x0, waiting for transfers between devices: 1070 us -> none  [combined_all(): pieces = jax.tree.map(lambda part: lax.all_gather(part, axis), value)]
    unnamed x1 -> x0, blocking collectives: 109 us -> none
    slice x11 -> x0, local copies, waits for them, and re-layouts: 105 us -> none  [the longest x6 97.7 us: combined_all(): tail = jax.tree.map(lambda part: part[1:], pieces)]
    pallas_call x0 -> x1, Pallas kernels: none -> 100 us  [per_device(): pl.pallas_call(functools.partial(kernel, (users, items, xn, zn, cyc, widt...]
    all_gather x2 -> x0, blocking collectives: 86.3 us -> none  [combined_all(): pieces = jax.tree.map(lambda part: lax.all_gather(part, axis), value)]
    add x14 -> x0, other arithmetic: 69.5 us -> none  [the longest x7 69.4 us: chan_combine(): moment_a + moment_b]
    dot_general x3 -> x0, matrix products: 32.1 us -> none  [contract_users(): lax.dot_general(left, right, (((0,), (0,)), ((), ())), preferred_element_...]
    psum x1 -> x0, waiting for transfers between devices: 24.4 us -> none  [from_root(): return lax.psum(block, axis)]
  transfers between devices with their start and end apart: 4 -> 0, of which waited for: 4 -> 0; matrix products, arithmetic and copies ran while one was open for 1% -> 0% of each run, Pallas kernels for 0% -> 0%
where the time goes in v1:
time: 109 us
  Pallas kernels  100 us (92%)
  other arithmetic  3.66 us (3%)
  local copies, waits for them, and re-layouts  3.63 us (3%)
  between operations  1.32 us (1%)
    pallas_call x1, Pallas kernels, per_device(): pl.pallas_call(functools.partial(kernel, (users, items, xn, zn, cyc, widt...  100 us
    unnamed x2, local copies, waits for them, and re-layouts  3.63 us
    select_n x1, other arithmetic, per_device(): jnp.where(lax.axis_index('items') == chosen // per_shard, local, jnp.zero...  2.38 us

profile of v1, /device:TPU:0, one launch (start us, length us, event | category | flops | bytes accessed | tf_op | source)
XLA Modules:
  0.0 108.7 jit_solution(12334373137982353468)
XLA Ops:
  1.3 1.3 %broadcast_in_dim.11 = f32[2048]{0:T(1024)} convert(bf16[2048]{0:T(1024)(128)(2,1)} %param.4) | non-fusion elementwise | flops 2048 | bytes 12288 | tf_op jit(solution)/shard_map/broadcast_in_dim | solution.py:295
  2.6 2.4 %dynamic-slice_select_fusion.loc_ref = bf16[2048,256]{1,0:T(8,128)(2,1)} fusion(bf16[2048,8192]{1,0:T(8,128)(2,1)} %x_ref.1, s32[]{:T(128)S(6)} %select_n.25, pred[]{:T(512)S(6)} %eq.5), kind=kLoop, calls=%fused_computation | loop fusion | flops 524288 | bytes 2097157 | tf_op jit(solution)/shard_map/jit(_where)/select_n | solution.py:294
  5.0 100.1 %panel_covariance.1 = (f32[32,32,256]{2,1,0:T(8,128)}, f32[4,8,32]{2,1,0:T(8,128)}) custom-call(bf16[2048,8192]{1,0:T(8,128)(2,1)} %x_ref.1, bf16[2048,256]{1,0:T(8,128)(2,1)} %dynamic-slice_select_fusion.loc_ref, f32[1,2048]{1,0:T(1,128)} %bitcast.7), custom_call_target="tpu_custom_call" | custom-call | flops 9126805504 | bytes 33554432 | tf_op jit(solution)/shard_map/panel_covariance/pallas_call | solution.py:301
  105.1 2.3 %copy.8 = f32[32,32,256]{2,1,0:T(8,128)} copy(f32[32,32,256]{2,1,0:T(8,128)} %get-tuple-element.8) | data formatting | bytes 2097152
  107.4 1.3 %copy.9 = f32[32,32]{1,0:T(8,128)} copy(f32[32,32]{1,0:T(8,128)} %bitcast.8) | data formatting | bytes 8192

commit v2 on v1

v2 whole, which is shorter than its diff:
```python
import functools
import math

import jax
import jax.numpy as jnp
from jax import lax
from jax.experimental import pallas as pl
from jax.experimental.pallas import tpu as pltpu
from jax.sharding import PartitionSpec as P

P_SIZE = 256
BLK = 32
EXTRA = 16
TILE = 256
PHASES = 2
COLS = P_SIZE // PHASES
PIECES = 2
LAG = 3
STEP = math.log(2.0) / 256.0
TOP = 32600.0
f32 = jnp.float32


def encode(block):
    top = jnp.max(jnp.abs(block), axis=0, keepdims=True)
    code = jnp.ceil(jnp.log(jnp.maximum(top, 1e-30)) * (1.0 / STEP)) + 1.0
    scaled = jnp.round(block * (jnp.exp(code * -STEP) * TOP))
    return scaled.astype(jnp.int32).astype(jnp.int16), code


def decode(codes, code):
    return codes.astype(jnp.int32).astype(f32) * (jnp.exp(code * STEP) * (1.0 / TOP))


def kernel(
    sizes, x_ref, loc_ref, w_ref, cov_ref, mean_ref,
    xbuf, turned, full, half, near, far, lhs, pmean, gram, own,
    xsend, xrecv, zsend, zrecv, icov, sums, sums_all, stat, stat_all, shift, mean_mine, mean_all,
    load_sem, near_s, near_r, far_s, far_r, back_s, back_r, xs, xr, zs, zr, is_, ir,
    sum_s, sum_r, stat_s, stat_r, mean_s, mean_r,
):
    users, items, xn, zn, cyc, width = sizes
    rows = loc_ref.shape[0]
    chunk = users * width
    user, item = lax.axis_index("users"), lax.axis_index("items")
    z, x = lax.div(user, xn), lax.rem(user, xn)
    y, core = lax.div(item, 2), lax.rem(item, 2)
    yn = items // 2
    units = PHASES * cyc

    def load(c):
        return pltpu.make_async_copy(x_ref.at[:, pl.ds(c * chunk, chunk)], xbuf.at[c], load_sem.at[c])

    def remote(src, dst, send, recv, to_user, to_item):
        return pltpu.make_async_remote_copy(
            src_ref=src, dst_ref=dst, send_sem=send, recv_sem=recv,
            device_id={"users": to_user, "items": to_item},
            device_id_type=pl.DeviceIdType.MESH,
        )

    for c in range(cyc):
        load(c).start()

    barrier = pltpu.get_barrier_semaphore()
    for d in range(1, users):
        pl.semaphore_signal(
            barrier, inc=1, device_id={"users": lax.rem(user + d, users), "items": item},
            device_id_type=pl.DeviceIdType.MESH,
        )
    for d in range(1, items):
        pl.semaphore_signal(
            barrier, inc=1, device_id={"users": user, "items": lax.rem(item + d, items)},
            device_id_type=pl.DeviceIdType.MESH,
        )
    for r in range(rows // TILE):
        part = pl.ds(r * TILE, TILE)
        turned[:, part] = loc_ref[part, :].astype(f32).T.astype(jnp.bfloat16)
    pl.semaphore_wait(barrier, users + items - 2)

    side = COLS // 2
    piece = side // PIECES

    def place(f, p, whose):
        return pl.ds(pl.multiple_of(f * COLS + whose * side + p * piece, piece), piece)

    def near_copy(f, p):
        n = f * PIECES + p
        return remote(turned.at[place(f, p, 1 - core)], near.at[n],
                      near_s.at[n], near_r.at[n], user, y * 2 + 1 - core)

    def far_copy(f, p, d):
        n = f * PIECES + p
        return remote(half.at[n], far.at[n, d - 1], far_s.at[n, d - 1], far_r.at[n, d - 1],
                      user, lax.rem(y + d, yn) * 2 + core)

    def back_copy(f, p):
        n = f * PIECES + p
        return remote(full.at[place(f, p, core)], full.at[place(f, p, core)],
                      back_s.at[n], back_r.at[n], user, y * 2 + 1 - core)

    def panel_back(f):
        for p in range(PIECES):
            value = half[f * PIECES + p]
            for d in range(1, yn):
                far_copy(f, p, d).wait_recv()
                value = value + far[f * PIECES + p, d - 1]
            full[place(f, p, core), :] = value
            back_copy(f, p).start()

    def panel_weigh(f):
        for p in range(PIECES):
            back_copy(f, p).wait_recv()
        weights = jnp.concatenate([w_ref[r : r + 1, :] for r in range(rows // 128)], axis=1).astype(f32)
        count = jnp.sum(weights, axis=1, keepdims=True)
        for r in range(0, COLS, 64):
            part = pl.ds(f * COLS + r, 64)
            product = full[part, :].astype(f32) * weights
            lhs[f, r : r + 64, :] = product.astype(jnp.bfloat16)
            pmean[part, :] = jnp.broadcast_to(jnp.sum(product, axis=1, keepdims=True), (64, 128))
        lhs[f, COLS : COLS + EXTRA, :] = jnp.broadcast_to(weights, (EXTRA, rows)).astype(jnp.bfloat16)
        part = pl.ds(f * COLS, COLS)
        stat[0:8, part] = pmean[part, :].T[0:8, :]
        stat[8:16, part] = jnp.broadcast_to(count, (8, COLS))
        pmean[part, :] = pmean[part, :] / count

    for f in range(PHASES):
        for p in range(PIECES):
            near_copy(f, p).start()
    for f in range(PHASES):
        for p in range(PIECES):
            near_copy(f, p).wait_recv()
            half[f * PIECES + p] = turned[place(f, p, core), :] + near[f * PIECES + p]
            for d in range(1, yn):
                far_copy(f, p, d).start()
    panel_back(0)
    panel_weigh(0)

    def stat_copy(d):
        return remote(stat, stat_all.at[user], stat_s.at[d - 1], stat_r.at[d - 1],
                      lax.rem(user + d, users), item)

    def sum_copy(d):
        peer = lax.rem(user + d, users)
        return remote(sums.at[peer], sums_all.at[user], sum_s.at[d - 1], sum_r.at[d - 1], peer, item)

    def mean_copy(d):
        return remote(mean_mine, mean_all.at[item], mean_s.at[d - 1], mean_r.at[d - 1],
                      user, lax.rem(item + d, items))

    def x_copy(n, d):
        return remote(xsend.at[n, d - 1], xrecv.at[n, d - 1], xs.at[n, d - 1], xr.at[n, d - 1],
                      z * xn + lax.rem(x + d, xn), item)

    def z_copy(n, d):
        return remote(zsend.at[n, d - 1], zrecv.at[n, d - 1], zs.at[n, d - 1], zr.at[n, d - 1],
                      lax.rem(z + d, zn) * xn + x, item)

    def item_copy(n, d):
        peer = lax.rem(item + d, items)
        f, c = lax.div(n, cyc), lax.rem(n, cyc)
        return remote(icov.at[n, pl.ds(pl.multiple_of(peer * BLK, BLK), BLK)],
                      cov_ref.at[item * cyc + c, :, pl.ds(pl.multiple_of(f * COLS, COLS), COLS)],
                      is_.at[n, d - 1], ir.at[n, d - 1], user, peer)

    def compute(n):
        f, c = lax.div(n, cyc), lax.rem(n, cyc)

        @pl.when(f == 0)
        def _():
            load(c).wait()

        mean = pmean[pl.ds(pl.multiple_of(f * COLS, COLS), COLS), 0:1]

        def tile(t, _):
            part = pl.ds(pl.multiple_of(t * TILE, TILE), TILE)
            value = jnp.dot(lhs[f], xbuf[c, :, part], preferred_element_type=f32)
            total = value[COLS : COLS + 1, :]
            gram[:, part] = value[0:COLS, :] - mean * total

            @pl.when(f == 0)
            def _():
                for b in range(TILE // width):
                    sums[t * (TILE // width) + b, pl.ds(c, 1), :] = total[:, b * width : (b + 1) * width]

            return 0

        lax.fori_loop(0, chunk // TILE, tile, 0)
        row = lax.broadcasted_iota(jnp.int32, (EXTRA, width), 0)
        for d in range(1, xn):
            scales = jnp.zeros((EXTRA, width), f32)
            for k in range(zn):
                start = pl.multiple_of((k * xn + lax.rem(x + d, xn)) * width, width)
                codes, code = encode(gram[:, pl.ds(start, width)])
                xsend[n, d - 1, k * COLS : (k + 1) * COLS, :] = codes
                scales = jnp.where(row == k, code, scales)
            xsend[n, d - 1, zn * COLS : zn * COLS + EXTRA, :] = scales.astype(jnp.int32).astype(jnp.int16)
            x_copy(n, d).start()
        for k in range(zn):
            start = pl.multiple_of((k * xn + x) * width, width)
            own[n, k] = gram[:, pl.ds(start, width)]

    def relay(n):
        for d in range(1, xn):
            x_copy(n, d).wait_recv()
            scales = xrecv[n, d - 1, zn * COLS : zn * COLS + EXTRA, :].astype(jnp.int32).astype(f32)
            for k in range(zn):
                codes = xrecv[n, d - 1, k * COLS : (k + 1) * COLS, :]
                own[n, k] = own[n, k] + decode(codes, scales[k : k + 1])
        for d in range(1, zn):
            codes, code = encode(own[n, lax.rem(z + d, zn)])
            zsend[n, d - 1, 0:COLS, :] = codes
            code = jnp.broadcast_to(code, (EXTRA, width))
            zsend[n, d - 1, COLS : COLS + EXTRA, :] = code.astype(jnp.int32).astype(jnp.int16)
            z_copy(n, d).start()

    def statistics():
        sums_all[user] = sums[user]
        stat_all[user] = stat[...]
        for d in range(1, users):
            stat_copy(d).wait_recv()
        whole = stat_all[0]
        for g in range(1, users):
            whole = whole + stat_all[g]
        panel_mean = whole[0:1, :] / whole[8:9, :]
        for g in range(users):
            delta = stat_all[g, 0:1, :] / stat_all[g, 8:9, :] - panel_mean
            shift[g] = jnp.broadcast_to(delta, (width, P_SIZE)).T
        for d in range(1, users):
            sum_copy(d).wait_recv()
        means = sums_all[0]
        for g in range(1, users):
            means = means + sums_all[g]
        mean_mine[...] = means / whole[8:9, 0:1]
        for d in range(1, items):
            mean_copy(d).start()
        mean_all[item] = mean_mine[...]

    def finish(n):
        f, c = lax.div(n, cyc), lax.rem(n, cyc)
        value = own[n, z]
        for g in range(users):
            part = pl.ds(pl.multiple_of(f * COLS, COLS), COLS)
            value = value + shift[g, part, :] * sums_all[g, pl.ds(c, 1), :]
        for d in range(1, zn):
            z_copy(n, d).wait_recv()
            code = zrecv[n, d - 1, COLS : COLS + EXTRA, :].astype(jnp.int32).astype(f32)[0:1]
            value = value + decode(zrecv[n, d - 1, 0:COLS, :], code)
        total = stat_all[0, 8:9, 0:1]
        for g in range(1, users):
            total = total + stat_all[g, 8:9, 0:1]
        icov[n] = (value / total).T
        for d in range(1, items):
            item_copy(n, d).start()
        part = pl.ds(pl.multiple_of(f * COLS, COLS), COLS)
        cov_ref[item * cyc + c, :, part] = icov[n, pl.ds(pl.multiple_of(item * BLK, BLK), BLK), :]

    lag = min(LAG, units)
    last = cyc + lag

    def step(s, _):
        @pl.when(s < units)
        def _():
            compute(s)

        @pl.when(s == min(1, cyc - 1))
        def _():
            for f in range(1, PHASES):
                panel_back(f)

        @pl.when(s == min(3, cyc - 1))
        def _():
            for f in range(1, PHASES):
                panel_weigh(f)
            for d in range(1, users):
                stat_copy(d).start()

        @pl.when(s == cyc - 1)
        def _():
            for d in range(1, users):
                sum_copy(d).start()

        @pl.when(s >= lag)
        def _():
            relay(s - lag)

        @pl.when(s == last)
        def _():
            statistics()

        @pl.when(s >= last)
        def _():
            for k in range(PHASES):
                finish((s - last) * PHASES + k)

        return 0

    lax.fori_loop(0, units + lag, step, 0)

    for d in range(1, items):
        mean_copy(d).wait()
    for i in range(items):
        value = jnp.zeros((mean_all.shape[1], BLK), f32)
        for k in range(items):
            value = jnp.where(item == k, mean_all[i, :, k * BLK : (k + 1) * BLK], value)
        mean_ref[i * cyc : (i + 1) * cyc, :] = value[0:cyc]

    for f in range(PHASES):
        for p in range(PIECES):
            near_copy(f, p).wait_send()
            back_copy(f, p).wait_send()
            for d in range(1, yn):
                far_copy(f, p, d).wait_send()
    for d in range(1, users):
        stat_copy(d).wait_send()
        sum_copy(d).wait_send()

    def drain(n, _):
        for d in range(1, xn):
            x_copy(n, d).wait_send()
        for d in range(1, zn):
            z_copy(n, d).wait_send()
        for d in range(1, items):
            item_copy(n, d).wait()
        return 0

    lax.fori_loop(0, units, drain, 0)


def per_device(interactions, user_weights, panel_index):
    rows, shard = interactions.shape
    users, items = lax.axis_size("users"), lax.axis_size("items")
    zn = 4 if users % 4 == 0 else 1
    xn = users // zn
    width = items * BLK
    cyc = shard // (users * width)
    cyc8 = -(-cyc // 8) * 8
    yn = items // 2
    per_shard = shard // P_SIZE
    chosen = panel_index[0]
    local = lax.dynamic_slice_in_dim(interactions, chosen % per_shard * P_SIZE, P_SIZE, 1)
    local = jnp.where(lax.axis_index("items") == chosen // per_shard, local, jnp.zeros_like(local))
    weights = user_weights.reshape(rows // 128, 128)

    bf16, i16 = jnp.bfloat16, jnp.int16
    piece, tall = COLS // 2 // PIECES, COLS + EXTRA
    pieces, units = PHASES * PIECES, PHASES * cyc
    dma = pltpu.SemaphoreType.DMA
    vmem = pl.BlockSpec(memory_space=pltpu.VMEM)
    cov, mean = pl.pallas_call(
        functools.partial(kernel, (users, items, xn, zn, cyc, width)),
        out_shape=(
            jax.ShapeDtypeStruct((items * cyc, BLK, P_SIZE), f32),
            jax.ShapeDtypeStruct((items * cyc, BLK), f32),
        ),
        in_specs=[pl.BlockSpec(memory_space=pl.ANY), vmem, vmem],
        out_specs=(vmem, vmem),
        scratch_shapes=[
            pltpu.VMEM((cyc, rows, users * width), bf16),
            pltpu.VMEM((P_SIZE, rows), bf16),
            pltpu.VMEM((P_SIZE, rows), bf16),
            pltpu.VMEM((pieces, piece, rows), bf16),
            pltpu.VMEM((pieces, piece, rows), bf16),
            pltpu.VMEM((pieces, yn - 1, piece, rows), bf16),
            pltpu.VMEM((PHASES, tall, rows), bf16),
            pltpu.VMEM((P_SIZE, 128), f32),
            pltpu.VMEM((COLS, users * width), f32),
            pltpu.VMEM((units, zn, COLS, width), f32),
            pltpu.VMEM((units, xn - 1, zn * COLS + EXTRA, width), i16),
            pltpu.VMEM((units, xn - 1, zn * COLS + EXTRA, width), i16),
            pltpu.VMEM((units, zn - 1, tall, width), i16),
            pltpu.VMEM((units, zn - 1, tall, width), i16),
            pltpu.VMEM((units, width, COLS), f32),
            pltpu.VMEM((users, cyc8, width), f32),
            pltpu.VMEM((users, cyc8, width), f32),
            pltpu.VMEM((16, P_SIZE), f32),
            pltpu.VMEM((users, 16, P_SIZE), f32),
            pltpu.VMEM((users, P_SIZE, width), f32),
            pltpu.VMEM((cyc8, width), f32),
            pltpu.VMEM((items, cyc8, width), f32),
            dma((cyc,)),
            dma((pieces,)), dma((pieces,)),
            dma((pieces, yn - 1)), dma((pieces, yn - 1)),
            dma((pieces,)), dma((pieces,)),
            dma((units, xn - 1)), dma((units, xn - 1)),
            dma((units, zn - 1)), dma((units, zn - 1)),
            dma((units, items - 1)), dma((units, items - 1)),
            dma((users - 1,)), dma((users - 1,)),
            dma((users - 1,)), dma((users - 1,)),
            dma((items - 1,)), dma((items - 1,)),
        ],
        compiler_params=pltpu.CompilerParams(
            collective_id=0, has_side_effects=True, vmem_limit_bytes=60 * 2**20
        ),
        cost_estimate=pl.CostEstimate(
            flops=2 * P_SIZE * rows * shard, bytes_accessed=2 * rows * shard, transcendentals=0
        ),
        name="panel_covariance",
    )(interactions, local, weights)
    return cov, mean


def solution(mesh):
    return jax.shard_map(
        per_device,
        mesh=mesh,
        in_specs=(P("users", "items"), P("users"), P()),
        out_specs=(P(None, ("users", "items"), None), P(None, ("users", "items"))),
        check_vma=False,
    )
```

time: 109 us -> 95 us (0.87)
  Pallas kernels: 100 us -> 87.4 us
  other arithmetic: 3.66 us -> 2.38 us
    pallas_call x1, Pallas kernels: 100 us -> 87.4 us  [per_device(): pl.pallas_call(functools.partial(kernel, (users, items, xn, zn, cyc, widt...]
    broadcast_in_dim x1 -> x0, other arithmetic: 1.29 us -> none  [per_device(): weights = user_weights.astype(f32)[None, :]]
where the time goes in v2:
time: 95 us; the launch traced here: 94.7 us
  Pallas kernels  87.4 us (92%)
  local copies, waits for them, and re-layouts  3.63 us (4%)
  other arithmetic  2.38 us (3%)
  between operations  1.32 us (1%)
    pallas_call x1, Pallas kernels, per_device(): pl.pallas_call(functools.partial(kernel, (users, items, xn, zn, cyc, widt...  87.4 us
    unnamed x2, local copies, waits for them, and re-layouts  3.63 us
    select_n x1, other arithmetic, per_device(): jnp.where(lax.axis_index('items') == chosen // per_shard, local, jnp.zero...  2.38 us

profile of v2, /device:TPU:0, one launch (start us, length us, event | category | flops | bytes accessed | tf_op | source)
XLA Modules:
  0.0 94.7 jit_solution(6801222418182706630)
XLA Ops:
  1.3 2.4 %dynamic-slice_select_fusion.loc_ref = bf16[2048,256]{1,0:T(8,128)(2,1)} fusion(bf16[2048,8192]{1,0:T(8,128)(2,1)} %x_ref.1, s32[]{:T(128)S(6)} %select_n.25, pred[]{:T(512)S(6)} %eq.5), kind=kLoop, calls=%fused_computation | loop fusion | flops 524288 | bytes 2097157 | tf_op jit(solution)/shard_map/jit(_where)/select_n | solution.py:341
  3.7 87.4 %panel_covariance.1 = (f32[32,32,256]{2,1,0:T(8,128)}, f32[32,32]{1,0:T(8,128)}) custom-call(bf16[2048,8192]{1,0:T(8,128)(2,1)} %x_ref.1, bf16[2048,256]{1,0:T(8,128)(2,1)} %dynamic-slice_select_fusion.loc_ref, bf16[16,128]{1,0:T(8,128)(2,1)} %bitcast.6), custom_call_target="tpu_custom_call" | custom-call | flops 8589934592 | bytes 33554432 | tf_op jit(solution)/shard_map/panel_covariance/pallas_call | solution.py:349
  91.1 2.3 %copy.8 = f32[32,32,256]{2,1,0:T(8,128)} copy(f32[32,32,256]{2,1,0:T(8,128)} %get-tuple-element.4) | data formatting | bytes 2097152
  93.4 1.3 %copy.9 = f32[32,32]{1,0:T(8,128)} copy(f32[32,32]{1,0:T(8,128)} %get-tuple-element.5) | data formatting | bytes 8192

commit v3 on v2

--- a/solution.py
+++ b/solution.py
@@ -12,6 +12,7 @@
 BLK = 32
 EXTRA = 16
 TILE = 256
+DOT = 1024
 PHASES = 2
 COLS = P_SIZE // PHASES
 PIECES = 2
@@ -171,20 +172,25 @@
 
         mean = pmean[pl.ds(pl.multiple_of(f * COLS, COLS), COLS), 0:1]
 
+        wide = min(chunk, DOT)
+
         def tile(t, _):
-            part = pl.ds(pl.multiple_of(t * TILE, TILE), TILE)
+            part = pl.ds(pl.multiple_of(t * wide, wide), wide)
             value = jnp.dot(lhs[f], xbuf[c, :, part], preferred_element_type=f32)
             total = value[COLS : COLS + 1, :]
             gram[:, part] = value[0:COLS, :] - mean * total
 
             @pl.when(f == 0)
             def _():
-                for b in range(TILE // width):
-                    sums[t * (TILE // width) + b, pl.ds(c, 1), :] = total[:, b * width : (b + 1) * width]
+                for b in range(wide // width):
+                    sums[t * (wide // width) + b, pl.ds(c, 1), :] = total[:, b * width : (b + 1) * width]
 
             return 0
 
-        lax.fori_loop(0, chunk // TILE, tile, 0)
+        if chunk == wide:
+            tile(0, 0)
+        else:
+            lax.fori_loop(0, chunk // wide, tile, 0)
         row = lax.broadcasted_iota(jnp.int32, (EXTRA, width), 0)
         for d in range(1, xn):
             scales = jnp.zeros((EXTRA, width), f32)
@@ -324,6 +330,30 @@
         return 0
 
     lax.fori_loop(0, units, drain, 0)
+
+
+def hand_over_kernel(cov_ref, mean_ref, cov_out, mean_out, sem):
+    whole = pltpu.make_async_copy(cov_ref, cov_out, sem.at[0])
+    means = pltpu.make_async_copy(mean_ref, mean_out, sem.at[1])
+    whole.start()
+    means.start()
+    whole.wait()
+    means.wait()
+
+
+def hand_over(cov, mean):
+    anywhere = pl.BlockSpec(memory_space=pl.ANY)
+    vmem = pl.BlockSpec(memory_space=pltpu.VMEM)
+    return pl.pallas_call(
+        hand_over_kernel,
+        out_shape=(
+            jax.ShapeDtypeStruct(cov.shape, f32), jax.ShapeDtypeStruct(mean.shape, f32),
+        ),
+        in_specs=[vmem, vmem],
+        out_specs=(anywhere, anywhere),
+        scratch_shapes=[pltpu.SemaphoreType.DMA((2,))],
+        name="hand_over",
+    )(cov, mean)
 
 
 def per_device(interactions, user_weights, panel_index):
@@ -396,7 +426,7 @@
         ),
         name="panel_covariance",
     )(interactions, local, weights)
-    return cov, mean
+    return hand_over(cov, mean)
 
 
 def solution(mesh):

time: 95 us -> 92.3 us (0.972)
  local copies, waits for them, and re-layouts: 3.63 us -> 0 us
  Pallas kernels: 87.4 us -> 88.4 us
    unnamed x2 -> x0, local copies, waits for them, and re-layouts: 3.63 us -> none
    pallas_call x0 -> x1, Pallas kernels: none -> 2.22 us  [hand_over(): pl.pallas_call(hand_over_kernel, out_shape=(jax.ShapeDtypeStruct(cov.shap...]
    pallas_call x1, Pallas kernels: 87.4 us -> 86.2 us  [per_device(): pl.pallas_call(functools.partial(kernel, (users, items, xn, zn, cyc, widt...]
where the time goes in v3:
time: 92.3 us; the launch traced here: 92.1 us
  Pallas kernels  88.4 us (96%)
  other arithmetic  2.38 us (3%)
  between operations  1.32 us (1%)
    pallas_call x1, Pallas kernels, per_device(): pl.pallas_call(functools.partial(kernel, (users, items, xn, zn, cyc, widt...  86.2 us
    select_n x1, other arithmetic, per_device(): jnp.where(lax.axis_index('items') == chosen // per_shard, local, jnp.zero...  2.38 us
    pallas_call x1, Pallas kernels, hand_over(): pl.pallas_call(hand_over_kernel, out_shape=(jax.ShapeDtypeStruct(cov.shap...  2.22 us

profile of v3, /device:TPU:0, one launch (start us, length us, event | category | flops | bytes accessed | tf_op | source)
XLA Modules:
  0.0 92.1 jit_solution(14954682905215485279)
XLA Ops:
  1.3 2.4 %dynamic-slice_select_fusion.loc_ref = bf16[2048,256]{1,0:T(8,128)(2,1)} fusion(bf16[2048,8192]{1,0:T(8,128)(2,1)} %x_ref.1, s32[]{:T(128)S(6)} %select_n.25, pred[]{:T(512)S(6)} %eq.5), kind=kLoop, calls=%fused_computation | loop fusion | flops 524288 | bytes 2097157 | tf_op jit(solution)/shard_map/jit(_where)/select_n | solution.py:371
  3.7 86.2 %panel_covariance.1 = (f32[32,32,256]{2,1,0:T(8,128)}, f32[32,32]{1,0:T(8,128)}) custom-call(bf16[2048,8192]{1,0:T(8,128)(2,1)} %x_ref.1, bf16[2048,256]{1,0:T(8,128)(2,1)} %dynamic-slice_select_fusion.loc_ref, bf16[16,128]{1,0:T(8,128)(2,1)} %bitcast.6), custom_call_target="tpu_custom_call" | custom-call | flops 8589934592 | bytes 33554432 | tf_op jit(solution)/shard_map/panel_covariance/pallas_call | solution.py:379
  89.9 2.2 %hand_over.1 = (f32[32,32,256]{2,1,0:T(8,128)}, f32[32,32]{1,0:T(8,128)}) custom-call(f32[32,32,256]{2,1,0:T(8,128)} %get-tuple-element.4.cov_ref, f32[32,32]{1,0:T(8,128)} %get-tuple-element.5.mean_ref), custom_call_target="tpu_custom_call" | custom-call | tf_op jit(solution)/shard_map/hand_over/pallas_call | solution.py:347

commit v4 on v3

--- a/solution.py
+++ b/solution.py
@@ -16,7 +16,7 @@
 PHASES = 2
 COLS = P_SIZE // PHASES
 PIECES = 2
-LAG = 3
+LAG = 2
 STEP = math.log(2.0) / 256.0
 TOP = 32600.0
 f32 = jnp.float32
@@ -152,9 +152,14 @@
         return remote(xsend.at[n, d - 1], xrecv.at[n, d - 1], xs.at[n, d - 1], xr.at[n, d - 1],
                       z * xn + lax.rem(x + d, xn), item)
 
-    def z_copy(n, d):
-        return remote(zsend.at[n, d - 1], zrecv.at[n, d - 1], zs.at[n, d - 1], zr.at[n, d - 1],
-                      lax.rem(z + d, zn) * xn + x, item)
+    def z_copy(n, block, slot, to):
+        return remote(zsend.at[n, block], zrecv.at[n, slot], zs.at[n, block], zr.at[n, slot],
+                      to * xn + x, item)
+
+    def z_arrived(n, slot):
+        z_copy(n, 0, slot, lax.rem(z + 1, zn)).wait_recv()
+        code = zrecv[n, slot, COLS : COLS + EXTRA, :].astype(jnp.int32).astype(f32)[0:1]
+        return decode(zrecv[n, slot, 0:COLS, :], code)
 
     def item_copy(n, d):
         peer = lax.rem(item + d, items)
@@ -212,12 +217,28 @@
             for k in range(zn):
                 codes = xrecv[n, d - 1, k * COLS : (k + 1) * COLS, :]
                 own[n, k] = own[n, k] + decode(codes, scales[k : k + 1])
-        for d in range(1, zn):
-            codes, code = encode(own[n, lax.rem(z + d, zn)])
-            zsend[n, d - 1, 0:COLS, :] = codes
-            code = jnp.broadcast_to(code, (EXTRA, width))
-            zsend[n, d - 1, COLS : COLS + EXTRA, :] = code.astype(jnp.int32).astype(jnp.int16)
-            z_copy(n, d).start()
+
+    def z_send(n, at, block, step_z):
+        value = own[n, block]
+        if 0 <= at - step_z < zn:
+            value = value + z_arrived(n, block)
+        codes, code = encode(value)
+        zsend[n, block, 0:COLS, :] = codes
+        code = jnp.broadcast_to(code, (EXTRA, width))
+        zsend[n, block, COLS : COLS + EXTRA, :] = code.astype(jnp.int32).astype(jnp.int16)
+        slot = zn if step_z < 0 and block == at - 1 else block
+        z_copy(n, block, slot, at + step_z).start()
+
+    def hop(n, h):
+        @pl.when(z == h)
+        def _():
+            for block in range(h + 1, zn):
+                z_send(n, h, block, 1)
+
+        @pl.when(z == zn - 1 - h)
+        def _():
+            for block in range(0, zn - 1 - h):
+                z_send(n, zn - 1 - h, block, -1)
 
     def statistics():
         sums_all[user] = sums[user]
@@ -243,14 +264,20 @@
 
     def finish(n):
         f, c = lax.div(n, cyc), lax.rem(n, cyc)
+        for k in range(zn):
+            @pl.when(z == k)
+            def _():
+                value = own[n, k]
+                if k > 0:
+                    value = value + z_arrived(n, k)
+                if k < zn - 1:
+                    value = value + z_arrived(n, zn)
+                own[n, k] = value
+
         value = own[n, z]
         for g in range(users):
             part = pl.ds(pl.multiple_of(f * COLS, COLS), COLS)
             value = value + shift[g, part, :] * sums_all[g, pl.ds(c, 1), :]
-        for d in range(1, zn):
-            z_copy(n, d).wait_recv()
-            code = zrecv[n, d - 1, COLS : COLS + EXTRA, :].astype(jnp.int32).astype(f32)[0:1]
-            value = value + decode(zrecv[n, d - 1, 0:COLS, :], code)
         total = stat_all[0, 8:9, 0:1]
         for g in range(1, users):
             total = total + stat_all[g, 8:9, 0:1]
@@ -261,7 +288,8 @@
         cov_ref[item * cyc + c, :, part] = icov[n, pl.ds(pl.multiple_of(item * BLK, BLK), BLK), :]
 
     lag = min(LAG, units)
-    last = cyc + lag
+    hops = zn - 1
+    last = cyc + lag + hops
 
     def step(s, _):
         @pl.when(s < units)
@@ -287,7 +315,14 @@
 
         @pl.when(s >= lag)
         def _():
-            relay(s - lag)
+            @pl.when(s < units + lag)
+            def _():
+                relay(s - lag)
+
+        for h in range(hops):
+            @pl.when((s >= lag + h) & (s < units + lag + h))
+            def _():
+                hop(s - lag - h, h)
 
         @pl.when(s == last)
         def _():
@@ -300,7 +335,7 @@
 
         return 0
 
-    lax.fori_loop(0, units + lag, step, 0)
+    lax.fori_loop(0, units + lag + hops, step, 0)
 
     for d in range(1, items):
         mean_copy(d).wait()
@@ -323,8 +358,10 @@
     def drain(n, _):
         for d in range(1, xn):
             x_copy(n, d).wait_send()
-        for d in range(1, zn):
-            z_copy(n, d).wait_send()
+        for k in range(zn):
+            @pl.when(z != k)
+            def _():
+                z_copy(n, k, k, lax.rem(z + 1, zn)).wait_send()
         for d in range(1, items):
             item_copy(n, d).wait()
         return 0
@@ -397,8 +434,8 @@
             pltpu.VMEM((units, zn, COLS, width), f32),
             pltpu.VMEM((units, xn - 1, zn * COLS + EXTRA, width), i16),
             pltpu.VMEM((units, xn - 1, zn * COLS + EXTRA, width), i16),
-            pltpu.VMEM((units, zn - 1, tall, width), i16),
-            pltpu.VMEM((units, zn - 1, tall, width), i16),
+            pltpu.VMEM((units, zn, tall, width), i16),
+            pltpu.VMEM((units, zn + 1, tall, width), i16),
             pltpu.VMEM((units, width, COLS), f32),
             pltpu.VMEM((users, cyc8, width), f32),
             pltpu.VMEM((users, cyc8, width), f32),
@@ -412,7 +449,7 @@
             dma((pieces, yn - 1)), dma((pieces, yn - 1)),
             dma((pieces,)), dma((pieces,)),
             dma((units, xn - 1)), dma((units, xn - 1)),
-            dma((units, zn - 1)), dma((units, zn - 1)),
+            dma((units, zn)), dma((units, zn + 1)),
             dma((units, items - 1)), dma((units, items - 1)),
             dma((users - 1,)), dma((users - 1,)),
             dma((users - 1,)), dma((users - 1,)),

time: 92.3 us -> 90 us (0.975)
  Pallas kernels: 88.4 us -> 86.1 us
    pallas_call x1, Pallas kernels: 86.2 us -> 83.9 us  [per_device(): pl.pallas_call(functools.partial(kernel, (users, items, xn, zn, cyc, widt...]
where the time goes in v4:
time: 90 us; the launch traced here: 89.8 us
  Pallas kernels  86.1 us (96%)
  other arithmetic  2.38 us (3%)
  between operations  1.32 us (1%)
    pallas_call x1, Pallas kernels, per_device(): pl.pallas_call(functools.partial(kernel, (users, items, xn, zn, cyc, widt...  83.9 us
    select_n x1, other arithmetic, per_device(): jnp.where(lax.axis_index('items') == chosen // per_shard, local, jnp.zero...  2.38 us
    pallas_call x1, Pallas kernels, hand_over(): pl.pallas_call(hand_over_kernel, out_shape=(jax.ShapeDtypeStruct(cov.shap...  2.22 us

profile of v4, /device:TPU:0, one launch (start us, length us, event | category | flops | bytes accessed | tf_op | source)
XLA Modules:
  0.0 89.8 jit_solution(1502457998051384442)
XLA Ops:
  1.3 2.4 %dynamic-slice_select_fusion.loc_ref = bf16[2048,256]{1,0:T(8,128)(2,1)} fusion(bf16[2048,8192]{1,0:T(8,128)(2,1)} %x_ref.1, s32[]{:T(128)S(6)} %select_n.25, pred[]{:T(512)S(6)} %eq.5), kind=kLoop, calls=%fused_computation | loop fusion | flops 524288 | bytes 2097157 | tf_op jit(solution)/shard_map/jit(_where)/select_n | solution.py:408
  3.7 83.9 %panel_covariance.1 = (f32[32,32,256]{2,1,0:T(8,128)}, f32[32,32]{1,0:T(8,128)}) custom-call(bf16[2048,8192]{1,0:T(8,128)(2,1)} %x_ref.1, bf16[2048,256]{1,0:T(8,128)(2,1)} %dynamic-slice_select_fusion.loc_ref, bf16[16,128]{1,0:T(8,128)(2,1)} %bitcast.6), custom_call_target="tpu_custom_call" | custom-call | flops 8589934592 | bytes 33554432 | tf_op jit(solution)/shard_map/panel_covariance/pallas_call | solution.py:416
  87.6 2.2 %hand_over.1 = (f32[32,32,256]{2,1,0:T(8,128)}, f32[32,32]{1,0:T(8,128)}) custom-call(f32[32,32,256]{2,1,0:T(8,128)} %get-tuple-element.4.cov_ref, f32[32,32]{1,0:T(8,128)} %get-tuple-element.5.mean_ref), custom_call_target="tpu_custom_call" | custom-call | tf_op jit(solution)/shard_map/hand_over/pallas_call | solution.py:384

commit v5 on v4

--- a/solution.py
+++ b/solution.py
@@ -17,6 +17,7 @@
 COLS = P_SIZE // PHASES
 PIECES = 2
 LAG = 2
+EVERY, FIRST = 8, 2
 STEP = math.log(2.0) / 256.0
 TOP = 32600.0
 f32 = jnp.float32
@@ -36,8 +37,8 @@
 def kernel(
     sizes, x_ref, loc_ref, w_ref, cov_ref, mean_ref,
     xbuf, turned, full, half, near, far, lhs, pmean, gram, own,
-    xsend, xrecv, zsend, zrecv, icov, sums, sums_all, stat, stat_all, shift, mean_mine, mean_all,
-    load_sem, near_s, near_r, far_s, far_r, back_s, back_r, xs, xr, zs, zr, is_, ir,
+    xsend, xrecv, late_send, late_recv, zsend, zrecv, icov, sums, sums_all, stat, stat_all, shift, mean_mine, mean_all,
+    load_sem, near_s, near_r, far_s, far_r, back_s, back_r, xs, xr, ls, lr, zs, zr, is_, ir,
     sum_s, sum_r, stat_s, stat_r, mean_s, mean_r,
 ):
     users, items, xn, zn, cyc, width = sizes
@@ -152,6 +153,17 @@
         return remote(xsend.at[n, d - 1], xrecv.at[n, d - 1], xs.at[n, d - 1], xr.at[n, d - 1],
                       z * xn + lax.rem(x + d, xn), item)
 
+    def z_first(n):
+        return lax.rem(n, EVERY) == FIRST
+
+    def beside(n, d):
+        return units + lax.div(n, EVERY) * (xn - 1) + d - 1
+
+    def late_copy(n, d):
+        i = lax.div(n, EVERY)
+        return remote(late_send.at[i, d - 1], late_recv.at[i, d - 1], ls.at[i, d - 1], lr.at[i, d - 1],
+                      z * xn + lax.rem(x + d, xn), item)
+
     def z_copy(n, block, slot, to):
         return remote(zsend.at[n, block], zrecv.at[n, slot], zs.at[n, block], zr.at[n, slot],
                       to * xn + x, item)
@@ -196,16 +208,27 @@
             tile(0, 0)
         else:
             lax.fori_loop(0, chunk // wide, tile, 0)
-        row = lax.broadcasted_iota(jnp.int32, (EXTRA, width), 0)
-        for d in range(1, xn):
-            scales = jnp.zeros((EXTRA, width), f32)
-            for k in range(zn):
-                start = pl.multiple_of((k * xn + lax.rem(x + d, xn)) * width, width)
-                codes, code = encode(gram[:, pl.ds(start, width)])
-                xsend[n, d - 1, k * COLS : (k + 1) * COLS, :] = codes
-                scales = jnp.where(row == k, code, scales)
-            xsend[n, d - 1, zn * COLS : zn * COLS + EXTRA, :] = scales.astype(jnp.int32).astype(jnp.int16)
-            x_copy(n, d).start()
+        @pl.when(z_first(n))
+        def _():
+            for d in range(1, xn):
+                for k in range(zn):
+                    start = pl.multiple_of((k * xn + lax.rem(x + d, xn)) * width, width)
+                    own[beside(n, d), k] = gram[:, pl.ds(start, width)]
+
+        @pl.when(jnp.logical_not(z_first(n)))
+        def _():
+            row = lax.broadcasted_iota(jnp.int32, (EXTRA, width), 0)
+            for d in range(1, xn):
+                scales = jnp.zeros((EXTRA, width), f32)
+                for k in range(zn):
+                    start = pl.multiple_of((k * xn + lax.rem(x + d, xn)) * width, width)
+                    codes, code = encode(gram[:, pl.ds(start, width)])
+                    xsend[n, d - 1, k * COLS : (k + 1) * COLS, :] = codes
+                    scales = jnp.where(row == k, code, scales)
+                scales = scales.astype(jnp.int32).astype(jnp.int16)
+                xsend[n, d - 1, zn * COLS : zn * COLS + EXTRA, :] = scales
+                x_copy(n, d).start()
+
         for k in range(zn):
             start = pl.multiple_of((k * xn + x) * width, width)
             own[n, k] = gram[:, pl.ds(start, width)]
@@ -235,10 +258,43 @@
             for block in range(h + 1, zn):
                 z_send(n, h, block, 1)
 
+            @pl.when(z_first(n))
+            def _():
+                for d in range(1, xn):
+                    for block in range(h + 1, zn):
+                        z_send(beside(n, d), h, block, 1)
+
         @pl.when(z == zn - 1 - h)
         def _():
             for block in range(0, zn - 1 - h):
                 z_send(n, zn - 1 - h, block, -1)
+
+            @pl.when(z_first(n))
+            def _():
+                for d in range(1, xn):
+                    for block in range(0, zn - 1 - h):
+                        z_send(beside(n, d), zn - 1 - h, block, -1)
+
+    def home(n):
+        for k in range(zn):
+            @pl.when(z == k)
+            def _():
+                value = own[n, k]
+                if k > 0:
+                    value = value + z_arrived(n, k)
+                if k < zn - 1:
+                    value = value + z_arrived(n, zn)
+                own[n, k] = value
+
+    def late(n):
+        for d in range(1, xn):
+            home(beside(n, d))
+            codes, code = encode(own[beside(n, d), z])
+            i = lax.div(n, EVERY)
+            late_send[i, d - 1, 0:COLS, :] = codes
+            code = jnp.broadcast_to(code, (EXTRA, width))
+            late_send[i, d - 1, COLS : COLS + EXTRA, :] = code.astype(jnp.int32).astype(jnp.int16)
+            late_copy(n, d).start()
 
     def statistics():
         sums_all[user] = sums[user]
@@ -264,15 +320,15 @@
 
     def finish(n):
         f, c = lax.div(n, cyc), lax.rem(n, cyc)
-        for k in range(zn):
-            @pl.when(z == k)
-            def _():
-                value = own[n, k]
-                if k > 0:
-                    value = value + z_arrived(n, k)
-                if k < zn - 1:
-                    value = value + z_arrived(n, zn)
-                own[n, k] = value
+        home(n)
+
+        @pl.when(z_first(n))
+        def _():
+            i = lax.div(n, EVERY)
+            for d in range(1, xn):
+                late_copy(n, d).wait_recv()
+                code = late_recv[i, d - 1, COLS : COLS + EXTRA, :].astype(jnp.int32).astype(f32)[0:1]
+                own[n, z] = own[n, z] + decode(late_recv[i, d - 1, 0:COLS, :], code)
 
         value = own[n, z]
         for g in range(users):
@@ -315,7 +371,7 @@
 
         @pl.when(s >= lag)
         def _():
-            @pl.when(s < units + lag)
+            @pl.when((s < units + lag) & jnp.logical_not(z_first(s - lag)))
             def _():
                 relay(s - lag)
 
@@ -323,6 +379,10 @@
             @pl.when((s >= lag + h) & (s < units + lag + h))
             def _():
                 hop(s - lag - h, h)
+
+        @pl.when((s >= lag + hops) & (s < units + lag + hops) & z_first(s - lag - hops))
+        def _():
+            late(s - lag - hops)
 
         @pl.when(s == last)
         def _():
@@ -356,12 +416,26 @@
         sum_copy(d).wait_send()
 
     def drain(n, _):
-        for d in range(1, xn):
-            x_copy(n, d).wait_send()
+        @pl.when(z_first(n))
+        def _():
+            for d in range(1, xn):
+                late_copy(n, d).wait_send()
+
+        @pl.when(jnp.logical_not(z_first(n)))
+        def _():
+            for d in range(1, xn):
+                x_copy(n, d).wait_send()
+
         for k in range(zn):
             @pl.when(z != k)
             def _():
                 z_copy(n, k, k, lax.rem(z + 1, zn)).wait_send()
+
+                @pl.when(z_first(n))
+                def _():
+                    for d in range(1, xn):
+                        z_copy(beside(n, d), k, k, lax.rem(z + 1, zn)).wait_send()
+
         for d in range(1, items):
             item_copy(n, d).wait()
         return 0
@@ -411,6 +485,8 @@
     bf16, i16 = jnp.bfloat16, jnp.int16
     piece, tall = COLS // 2 // PIECES, COLS + EXTRA
     pieces, units = PHASES * PIECES, PHASES * cyc
+    firsts = (units + EVERY - 1 - FIRST) // EVERY
+    chains, firsts = units + firsts * (xn - 1), max(firsts, 1)
     dma = pltpu.SemaphoreType.DMA
     vmem = pl.BlockSpec(memory_space=pltpu.VMEM)
     cov, mean = pl.pallas_call(
@@ -431,11 +507,13 @@
             pltpu.VMEM((PHASES, tall, rows), bf16),
             pltpu.VMEM((P_SIZE, 128), f32),
             pltpu.VMEM((COLS, users * width), f32),
-            pltpu.VMEM((units, zn, COLS, width), f32),
+            pltpu.VMEM((chains, zn, COLS, width), f32),
             pltpu.VMEM((units, xn - 1, zn * COLS + EXTRA, width), i16),
             pltpu.VMEM((units, xn - 1, zn * COLS + EXTRA, width), i16),
-            pltpu.VMEM((units, zn, tall, width), i16),
-            pltpu.VMEM((units, zn + 1, tall, width), i16),
+            pltpu.VMEM((firsts, xn - 1, tall, width), i16),
+            pltpu.VMEM((firsts, xn - 1, tall, width), i16),
+            pltpu.VMEM((chains, zn, tall, width), i16),
+            pltpu.VMEM((chains, zn + 1, tall, width), i16),
             pltpu.VMEM((units, width, COLS), f32),
             pltpu.VMEM((users, cyc8, width), f32),
             pltpu.VMEM((users, cyc8, width), f32),
@@ -449,14 +527,15 @@
             dma((pieces, yn - 1)), dma((pieces, yn - 1)),
             dma((pieces,)), dma((pieces,)),
             dma((units, xn - 1)), dma((units, xn - 1)),
-            dma((units, zn)), dma((units, zn + 1)),
+            dma((firsts, xn - 1)), dma((firsts, xn - 1)),
+            dma((chains, zn)), dma((chains, zn + 1)),
             dma((units, items - 1)), dma((units, items - 1)),
             dma((users - 1,)), dma((users - 1,)),
             dma((users - 1,)), dma((users - 1,)),
             dma((items - 1,)), dma((items - 1,)),
         ],
         compiler_params=pltpu.CompilerParams(
-            collective_id=0, has_side_effects=True, vmem_limit_bytes=60 * 2**20
+            collective_id=0, has_side_effects=True, vmem_limit_bytes=61 * 2**20
         ),
         cost_estimate=pl.CostEstimate(
             flops=2 * P_SIZE * rows * shard, bytes_accessed=2 * rows * shard, transcendentals=0

time: 90 us -> 91.9 us (1.021)
  Pallas kernels: 86.1 us -> 88 us
    pallas_call x1, Pallas kernels: 83.9 us -> 85.8 us  [per_device(): pl.pallas_call(functools.partial(kernel, (users, items, xn, zn, cyc, widt...]
where the time goes in v5:
time: 91.9 us; the launch traced here: 91.7 us
  Pallas kernels  88 us (96%)
  other arithmetic  2.38 us (3%)
  between operations  1.32 us (1%)
    pallas_call x1, Pallas kernels, per_device(): pl.pallas_call(functools.partial(kernel, (users, items, xn, zn, cyc, widt...  85.8 us
    select_n x1, other arithmetic, per_device(): jnp.where(lax.axis_index('items') == chosen // per_shard, local, jnp.zero...  2.38 us
    pallas_call x1, Pallas kernels, hand_over(): pl.pallas_call(hand_over_kernel, out_shape=(jax.ShapeDtypeStruct(cov.shap...  2.22 us

profile of v5, /device:TPU:0, one launch (start us, length us, event | category | flops | bytes accessed | tf_op | source)
XLA Modules:
  0.0 91.7 jit_solution(12299882035082359232)
XLA Ops:
  1.3 2.4 %dynamic-slice_select_fusion.loc_ref = bf16[2048,256]{1,0:T(8,128)(2,1)} fusion(bf16[2048,8192]{1,0:T(8,128)(2,1)} %x_ref.1, s32[]{:T(128)S(6)} %select_n.25, pred[]{:T(512)S(6)} %eq.5), kind=kLoop, calls=%fused_computation | loop fusion | flops 524288 | bytes 2097157 | tf_op jit(solution)/shard_map/jit(_where)/select_n | solution.py:482
  3.7 85.8 %panel_covariance.1 = (f32[32,32,256]{2,1,0:T(8,128)}, f32[32,32]{1,0:T(8,128)}) custom-call(bf16[2048,8192]{1,0:T(8,128)(2,1)} %x_ref.1, bf16[2048,256]{1,0:T(8,128)(2,1)} %dynamic-slice_select_fusion.loc_ref, bf16[16,128]{1,0:T(8,128)(2,1)} %bitcast.6), custom_call_target="tpu_custom_call" | custom-call | flops 8589934592 | bytes 33554432 | tf_op jit(solution)/shard_map/panel_covariance/pallas_call | solution.py:492
  89.5 2.2 %hand_over.1 = (f32[32,32,256]{2,1,0:T(8,128)}, f32[32,32]{1,0:T(8,128)}) custom-call(f32[32,32,256]{2,1,0:T(8,128)} %get-tuple-element.4.cov_ref, f32[32,32]{1,0:T(8,128)} %get-tuple-element.5.mean_ref), custom_call_target="tpu_custom_call" | custom-call | tf_op jit(solution)/shard_map/hand_over/pallas_call | solution.py:458
